TPU v7x, 32 devices: a whole 2x2x4 slice. The times are simulated.
32 devices in a mesh: wide: 16 (over z, y, x), narrow: 2 (over core).
Axes of the slice: x: 2, y: 2, z: 4, core: 2. Of those that a mesh axis runs over, the one named last changes fastest.
Arguments:
- tokens: bfloat16 [16384, 2048], P('wide', 'narrow'), may hold values from -6 to 6
- attn_gain: bfloat16 [2048], replicated, may hold values from 0.5 to 1.5
- q_weight: bfloat16 [2048, 3072], P('wide', 'narrow'), may hold values from -6 to 6
- kva_weight: bfloat16 [2048, 576], P('wide'), may hold values from -0.125 to 0.125
- kv_gain: bfloat16 [512], replicated, may hold values from 0.5 to 1.5
- kvb_weight: bfloat16 [512, 4096], P(None, 'narrow'), may hold values from -0.25 to 0.25
- o_weight: bfloat16 [2048, 2048], P('narrow'), may hold values from -0.125 to 0.125
- adapter_down: bfloat16 [2048, 1024], P(None, 'narrow'), may hold values from -0.125 to 0.125
- adapter_up_weight: bfloat16 [1024, 3072], P(None, 'narrow'), may hold values from -1.5 to 1.5
- lengths: int32 [16, 4], P('wide'), may hold values from 1 to 512, 1024 in all within a row
- adapter_ids: int32 [16, 4], P('wide'), may hold values from 0 to 63
- adapter_slot: int32 [64], replicated, may hold values from 0 to 63, each once
Outputs:
- hidden: bfloat16 [16384, 2048], P('wide', 'narrow')
- latent_cache: bfloat16 [16384, 576], P('wide')
Inputs may be any that keep to these rules, and one draw needn't show every extreme that they name: Each row of lengths sums to 1024, and its longest prompt is exactly 512.
All inputs are finite; a program needn't handle non-finite values.
Results may differ from a plain program's by a relative error of at most 0.0095.
The roundings to bfloat16 on the way count: a program that leaves them out, or rounds other values in their place, can miss the bound.
Values may be sent and summed in bfloat16 or wider, within the bound.
A program may use at most 192 MiB of HBM per device.

v0:
```python
import jax
import jax.numpy as jnp
from jax import lax
from jax.sharding import PartitionSpec as P

NOPE = 128
ROPE = 64
VDIM = 128
LATENT = 512
RANK = 16


EPS = 1e-06
THETA = 50000.0
ADAPTER_SCALE = 2.0


def rms_scale(values, gain):
    mean_sq = jnp.mean(values * values, axis=-1, keepdims=True)
    return values * lax.rsqrt(mean_sq + EPS) * gain.astype(jnp.float32)


def rotate(values, positions):
    half = values.shape[-1] // 2
    freqs = jnp.exp(-jnp.log(THETA) * 2.0 * jnp.arange(half).astype(jnp.float32) / (2 * half))
    angle = positions.astype(jnp.float32)[:, None] * freqs[None, :]
    cosine = jnp.cos(angle)
    sine = jnp.sin(angle)
    if values.ndim == 3:
        cosine = cosine[:, None, :]
        sine = sine[:, None, :]
    first = values[..., :half]
    second = values[..., half:]
    return jnp.concatenate(
        [first * cosine - second * sine, first * sine + second * cosine], axis=-1
    )


def token_tables(length_row, id_row, adapter_slot, local_pos):
    ends = jnp.cumsum(length_row)
    starts = ends - length_row
    prompt = jnp.sum((ends[None, :] <= local_pos[:, None]).astype(jnp.int32), axis=1)
    onehot = (prompt[:, None] == jnp.arange(length_row.shape[0])[None, :]).astype(jnp.int32)
    position = local_pos - jnp.sum(onehot * starts[None, :], axis=1)
    adapter = jnp.sum(onehot * id_row[None, :], axis=1)
    slot_hot = (adapter[:, None] == jnp.arange(adapter_slot.shape[0])[None, :]).astype(jnp.int32)
    slot = jnp.sum(slot_hot * adapter_slot[None, :], axis=1)
    return (prompt, position, adapter, slot)


def pick_columns(stored, first_slots, prompts_here):
    blocks = [
        lax.dynamic_slice_in_dim(stored, first_slots[prompt_index] * RANK, RANK, 1)
        for prompt_index in range(prompts_here)
    ]
    return jnp.concatenate(blocks, axis=1)


def body(
    tokens,
    attn_gain,
    q_weight,
    kva_weight,
    kv_gain,
    kvb_weight,
    o_weight,
    adapter_down,
    adapter_up_weight,
    lengths,
    adapter_ids,
    adapter_slot,
):
    rows = tokens.shape[0]
    owned = adapter_down.shape[1] // RANK
    heads_here = o_weight.shape[0] // VDIM
    prompts_here = lengths.shape[1]
    whole = lax.all_gather(tokens, "narrow", axis=1, tiled=True)
    normed = rms_scale(whole.astype(jnp.float32), attn_gain).astype(jnp.bfloat16)
    local_pos = jnp.arange(rows)
    prompt, position, adapter, slot = token_tables(
        lengths[0], adapter_ids[0], adapter_slot, local_pos
    )
    query_vectors = jnp.dot(
        normed,
        lax.all_gather(q_weight, "wide", axis=0, tiled=True),
        preferred_element_type=jnp.float32,
    )
    kv_pre = jnp.dot(
        normed,
        lax.all_gather(kva_weight, "wide", axis=0, tiled=True),
        preferred_element_type=jnp.float32,
    )
    prompt_ids = adapter_ids[0]
    id_hot = (prompt_ids[:, None] == jnp.arange(adapter_slot.shape[0])[None, :]).astype(jnp.int32)
    prompt_position_slot = jnp.sum(id_hot * adapter_slot[None, :], axis=1)
    member = (prompt[:, None] == jnp.arange(prompts_here)[None, :]).astype(jnp.float32)
    mine = lax.axis_index("narrow")
    local_slot = prompt_position_slot - mine * owned
    held = ((local_slot >= 0) & (local_slot < owned)).astype(jnp.float32)
    safe_slot = jnp.clip(local_slot, 0, owned - 1)
    chosen = pick_columns(adapter_down, safe_slot, prompts_here)
    low = jnp.dot(normed, chosen, preferred_element_type=jnp.float32).reshape(
        rows, prompts_here, RANK
    )
    share = member * held[None, :]
    partial_low = jnp.sum(low * share[:, :, None], axis=1)
    lowrank = lax.psum(partial_low.astype(jnp.bfloat16), "narrow")
    up_blocks = [
        lax.dynamic_slice_in_dim(adapter_up_weight, prompt_ids[prompt_index] * RANK, RANK, 0)
        for prompt_index in range(prompts_here)
    ]
    up_weight_rows = jnp.concatenate(up_blocks, axis=0)
    spread_rows = (member.astype(jnp.bfloat16)[:, :, None] * lowrank[:, None, :]).reshape(
        rows, prompts_here * RANK
    )
    query_vectors = query_vectors + ADAPTER_SCALE * jnp.dot(
        spread_rows, up_weight_rows, preferred_element_type=jnp.float32
    )
    query_vectors = query_vectors.reshape(rows, heads_here, NOPE + ROPE)
    query_vectors = jnp.concatenate(
        [query_vectors[..., :NOPE], rotate(query_vectors[..., NOPE:], position)], axis=-1
    ).astype(jnp.bfloat16)
    latent = rms_scale(kv_pre[:, :LATENT], kv_gain).astype(jnp.bfloat16)
    key_rope = rotate(kv_pre[:, LATENT:], position).astype(jnp.bfloat16)
    latent_cache = jnp.concatenate([latent, key_rope], axis=1)
    expanded = jnp.dot(latent, kvb_weight, preferred_element_type=jnp.float32).astype(jnp.bfloat16)
    expanded = expanded.reshape(rows, heads_here, NOPE + VDIM)
    key_nope = expanded[..., :NOPE]
    values = expanded[..., NOPE:]
    scale = 1.0 / jnp.sqrt(jnp.float32(NOPE + ROPE))
    scores = jnp.einsum(
        "qhd,khd->hqk", query_vectors[..., :NOPE], key_nope, preferred_element_type=jnp.float32
    )
    scores = scores + jnp.einsum(
        "qhd,kd->hqk", query_vectors[..., NOPE:], key_rope, preferred_element_type=jnp.float32
    )
    scores = scores * scale
    allowed = (prompt[None, :] == prompt[:, None]) & (local_pos[None, :] <= local_pos[:, None])
    scores = jnp.where(allowed[None, :, :], scores, jnp.float32(-1e30))
    top = jnp.max(scores, axis=-1, keepdims=True)
    expo = jnp.exp(scores - top)
    weights = (expo / jnp.sum(expo, axis=-1, keepdims=True)).astype(jnp.bfloat16)
    attended = jnp.einsum(
        "hqk,khd->qhd", weights, values, preferred_element_type=jnp.float32
    ).astype(jnp.bfloat16)
    attended = attended.reshape(rows, heads_here * VDIM)
    partial_out = jnp.dot(attended, o_weight, preferred_element_type=jnp.float32)
    projected = lax.psum_scatter(
        partial_out.astype(jnp.bfloat16), "narrow", scatter_dimension=1, tiled=True
    ).astype(jnp.float32)
    hidden = (tokens.astype(jnp.float32) + projected).astype(jnp.bfloat16)
    return (hidden, latent_cache)


def solution(mesh):
    return jax.shard_map(
        body,
        mesh=mesh,
        in_specs=(
            P("wide", "narrow"),
            P(),
            P("wide", "narrow"),
            P("wide", None),
            P(),
            P(None, "narrow"),
            P("narrow", None),
            P(None, "narrow"),
            P(None, "narrow"),
            P("wide", None),
            P("wide", None),
            P(),
        ),
        out_specs=(P("wide", "narrow"), P("wide", None)),
        check_vma=False,
    )
```

profile of v0, /device:TPU:8, one launch (start us, length us, event | category | flops | bytes accessed | tf_op | source)
XLA Modules:
  0.0 295.6 jit_solution(16251947245194924016)
XLA Ops:
  7.2 0.0 copy-start
  7.2 0.0 all-gather.4.cloned.1.call-start
  7.2 0.7 all-gather.4.cloned.1.call-update
  7.9 0.0 all-gather.6.cloned.1.call-start
  8.0 0.7 all-gather.6.cloned.1.call-update
  8.7 0.0 all-gather.8.cloned.1.call-start
  8.7 0.7 all-gather.8.cloned.1.call-update
  9.4 0.0 reduce-scatter.2.cloned.1.call-start
  9.4 0.9 select_reduce_fusion.1
  10.3 0.7 fusion.46
  13.6 1.4 fusion.45
  17.6 0.8 reduce-window.4
  18.4 0.7 convert_element_type.90
  19.1 0.7 convert_element_type.88
  19.8 0.6 multiply_exponential_fusion
  20.4 0.1 convert_reduce_fusion
  20.5 0.7 fusion.35
  21.1 0.1 select_reduce_fusion
  21.3 0.1 fusion.34
  21.3 1.6 constant_dynamic-slice_fusion.3
  23.0 3.5 %constant_dynamic-slice_fusion.7 = (bf16[2048,16]{1,0:T(8,128)(2,1)}, bf16[2048,16]{1,0:T(8,128)(2,1)}, bf16[2048,16]{1,0:T(8,128)(2,1)}, bf16[2048,16]{1,0:T(8,128)(2,1)}) fusion(bf16[2048,512]{1,0:T(8,128)(2,1)} %param.19, s32[]{:T(128)S(6)} %select_n.28, s32[]{:T(128)S(6)} %select_n.29, s32[]{:T(128)S(6)} %select_n.31, s32[]{:T(128)S(6)} %select_n.30), kind=kLoop, calls=%fused_computation.73 | loop fusion | bytes 524304 | tf_op jit(solution)/shard_map/dynamic_slice | solution.py:53
  26.5 0.6 fusion.7
  27.1 0.0 all-gather.4.cloned.1.call-done
  27.1 0.0 copy-start.2
  27.1 3.2 %fusion.4 = f32[1024]{0:T(1024)S(1)} fusion(bf16[1024,2048]{1,0:T(8,128)(2,1)} %all-gather.4.cloned.1.call-done), kind=kLoop, calls=%fused_computation.9 | loop fusion | flops 6290432 | bytes 4198400 | tf_op jit(solution)/shard_map/reduce_sum | solution.py:19
  30.4 0.2 copy-done.2
  30.6 3.6 %fusion.17 = f32[1024,64]{0,1:T(8,128)S(1)} fusion(bf16[2048,16]{1,0:T(8,128)(2,1)} %get-tuple-element.14, bf16[2048,16]{1,0:T(8,128)(2,1)} %get-tuple-element.15, bf16[2048,16]{1,0:T(8,128)(2,1)} %get-tuple-element.13, bf16[2048,16]{1,0:T(8,128)(2,1)} %get-tuple-element.12, bf16[1024,2048]{1,0:T(8,128)(2,1)S(1)} %copy-done.2, ...), kind=kOutput, calls=%fused_computation.31 | convolution fusion | flops 277872640 | bytes 4730880 | tf_op jit(solution)/shard_map/dot_general | solution.py:102
  34.2 3.6 %psum.7 = bf16[1024,16]{0,1:T(8,128)(2,1)S(1)} all-reduce(bf16[1024,16]{0,1:T(8,128)(2,1)S(1)} %multiply_reduce_fusion.1), channel_id=1, replica_groups=mesh['wide'=16,'narrow'=2] {'narrow'}, use_global_device_ids=true, to_apply=%region_6.7 | all-reduce | flops 16384 | bytes 65536 | tf_op jit(solution)/shard_map/psum | solution.py:107
  37.8 55.3 %all-gather.6.cloned.1.call-done = bf16[2048,576]{0,1:T(8,128)(2,1)} async-done(((bf16[128,576]{0,1:T(8,128)(2,1)}), bf16[2048,576]{0,1:T(8,128)(2,1)}) %all-gather.6.cloned.1.call-update) | async-done | bytes 2359312 | tf_op jit(solution)/shard_map/all_gather | solution.py:90
  93.1 5.6 %fusion.42 = f32[1024,576]{0,1:T(8,128)S(1)} fusion(bf16[2048,576]{0,1:T(8,128)(2,1)} %all-gather.6.cloned.1.call-done, bf16[1024,2048]{1,0:T(8,128)(2,1)} %all-gather.4.cloned.1.call-done, f32[2048]{0:T(1024)S(1)} %convert_element_type.88, f32[1024]{0:T(1024)S(1)} %add_rsqrt_fusion.1), kind=kOutput, calls=%fused_computation.83 | convolution fusion | flops 2424307712 | bytes 8925184 | tf_op jit(solution)/shard_map/dot_general | solution.py:88
  98.7 0.2 multiply_reduce_fusion
  98.9 0.2 multiply_convert_fusion
  99.1 0.0 copy-done
  99.1 0.0 copy-start.3
  99.1 2.4 convolution_convert_fusion
  101.5 0.0 copy-done.3
  101.5 0.0 copy-start.10
  101.5 1.5 copy.40
  103.0 0.0 copy-done.10
  103.0 1.2 subtract_convert_fusion.1
  104.2 1.6 fusion.44
  105.8 83.6 %all-gather.8.cloned.1.call-done = bf16[2048,1536]{1,0:T(8,128)(2,1)} async-done(((bf16[128,1536]{1,0:T(8,128)(2,1)}), bf16[2048,1536]{1,0:T(8,128)(2,1)}) %all-gather.8.cloned.1.call-update) | async-done | bytes 6291472 | tf_op jit(solution)/shard_map/all_gather | solution.py:85
  189.4 0.0 copy-start.6
  189.4 0.0 copy-start.7
  189.4 0.0 copy-start.8
  189.4 10.1 %fusion.40 = f32[1024,1536]{1,0:T(8,128)S(1)} fusion(bf16[2048,1536]{1,0:T(8,128)(2,1)} %all-gather.8.cloned.1.call-done, bf16[1024,2048]{1,0:T(8,128)(2,1)} %all-gather.4.cloned.1.call-done, f32[2048]{0:T(1024)S(1)} %convert_element_type.88, f32[1024]{0:T(1024)S(1)} %add_rsqrt_fusion.1), kind=kOutput, calls=%fused_computation.82 | convolution fusion | flops 6450839552 | bytes 16789504 | tf_op jit(solution)/shard_map/dot_general | solution.py:83
  199.6 0.0 copy-done.6
  199.6 0.0 copy-done.7
  199.6 0.0 copy-done.8
  199.6 0.0 copy-done.9
  199.6 3.7 %multiply_add_fusion = f32[1024,1536]{1,0:T(8,128)} fusion(f32[1024,1536]{1,0:T(8,128)S(1)} %fusion.40, bf16[1024,64]{0,1:T(8,128)(2,1)S(1)} %bitcast.47, bf16[16,1536]{1,0:T(8,128)(2,1)S(1)} %copy-done.8, bf16[16,1536]{1,0:T(8,128)(2,1)S(1)} %copy-done.9, bf16[16,1536]{1,0:T(8,128)(2,1)S(1)} %copy-done.7, bf16[16,1536]{1,0:T(8,128)(2,1)S(1)} %copy-done.6), kind=kOutput, calls=%fused_computation.12 | convolution fusion | flops 205258752 | bytes 12910592 | tf_op jit(solution)/shard_map/dot_general | solution.py:116
  203.3 6.7 %copy.32 = f32[1024,1536]{0,1:T(8,128)} copy(f32[1024,1536]{1,0:T(8,128)} %multiply_add_fusion) | data formatting | bytes 12582912 | tf_op jit(solution)/shard_map/add | solution.py:116
  209.9 0.0 copy-done.5
  209.9 1.9 subtract_convert_fusion
  211.8 13.4 %fusion.13 = f32[1024,1024,8]{1,0,2:T(8,128)} fusion(bf16[1024,8,32]{0,2,1:T(8,128)(2,1)S(1)} %get-tuple-element.3, bf16[1024,8,32]{0,2,1:T(8,128)(2,1)S(1)} %get-tuple-element.2, bf16[1024,32]{0,1:T(8,128)(2,1)S(1)} %get-tuple-element.11, bf16[1024,32]{0,1:T(8,128)(2,1)S(1)} %get-tuple-element.10), kind=kOutput, calls=%fused_computation.25 | convolution fusion | flops 1076101120 | bytes 34734080 | tf_op jit(solution)/shard_map/qhd,kd->hqk/dot_general | solution.py:134
  225.2 26.8 %fusion.47 = (f32[8,1024]{1,0:T(8,128)S(1)}, f32[8,1024,1024]{1,2,0:T(8,128)}) fusion(f32[1024,1024,8]{1,0,2:T(8,128)} %fusion.13, pred[1024,1024]{0,1:T(8,128)(4,1)S(1)} %fusion.7, f32[1024,8,192]{0,2,1:T(8,128)} %bitcast.44, bf16[1024,8,128]{2,1,0:T(8,128)(2,1)S(1)} %get-tuple-element.5), kind=kOutput, calls=%fused_computation.87 | convolution fusion | flops 2189427712 | bytes 72384512 | tf_op jit(solution)/shard_map/sub | solution.py:141
  252.0 12.7 %fusion.10 = bf16[8,128,1024]{2,1,0:T(8,128)(2,1)S(1)} fusion(f32[8,1024,1024]{1,2,0:T(8,128)} %get-tuple-element.27, f32[8,1024]{1,0:T(8,128)S(1)} %get-tuple-element.26, bf16[1024,8,128]{2,1,0:T(8,128)(2,1)} %get-tuple-element.4), kind=kOutput, calls=%fused_computation.23 | convolution fusion | flops 2165309440 | bytes 37781504 | tf_op jit(solution)/shard_map/hqk,khd->qhd/dot_general | solution.py:143
  264.7 8.3 %convolution_convert_fusion.1 = bf16[1024,2048]{1,0:T(8,128)(2,1)} fusion(bf16[1024,1024]{0,1:T(8,128)(2,1)S(1)} %bitcast.52, bf16[1024,2048]{1,0:T(8,128)(2,1)} %param.18), kind=kOutput, calls=%fused_computation.18 | convolution fusion | flops 4297064448 | bytes 10485760 | tf_op jit(solution)/shard_map/dot_general | solution.py:147
  273.0 0.0 reduce-scatter.2.cloned.1.call-update
  273.0 1.2 copy-done.4
  274.2 1.1 pad_maximum_fusion
  275.3 9.2 %reduce-scatter.2.cloned.1.call-done = bf16[1024,1024]{1,0:T(8,128)(2,1)} async-done(((bf16[1024,2048]{1,0:T(8,128)(2,1)}), bf16[1024,1024]{1,0:T(8,128)(2,1)}) %reduce-scatter.2.cloned.1.call-update) | async-done | bytes 2097168 | tf_op jit(solution)/shard_map/reduce_scatter | solution.py:148
  284.5 4.5 %add_convert_fusion = bf16[1024,1024]{1,0:T(8,128)(2,1)} fusion(bf16[1024,1024]{1,0:T(8,128)(2,1)} %reduce-scatter.2.cloned.1.call-done, bf16[1024,1024]{1,0:T(8,128)(2,1)} %param.12), kind=kLoop, calls=%fused_computation.14 | loop fusion | flops 4194304 | bytes 6291456 | tf_op jit(solution)/shard_map/convert_element_type | solution.py:151
  289.0 0.0 copy-done.1
  (12 shorter events, 0.1 us)
Async XLA Ops:
  7.2 91.9 %copy-start = (bf16[512,2048]{1,0:T(8,128)(2,1)S(1)}, bf16[512,2048]{1,0:T(8,128)(2,1)}, u32[]{:S(2)}) copy-start(bf16[512,2048]{1,0:T(8,128)(2,1)} %param.17) | copy-start | bytes 6291460
  7.2 19.9 %all-gather.4.cloned.1.call-start = ((), (), s32[]{:S(2)}) async-start(), calls=%async_computation.1 | async-start | bytes 6291456 | tf_op jit(solution)/shard_map/all_gather | solution.py:77
  7.9 85.1 %all-gather.6.cloned.1.call-start = ((), (), s32[]{:S(2)}) async-start(), calls=%async_computation.2 | async-start | bytes 2506752 | tf_op jit(solution)/shard_map/all_gather | solution.py:90
  8.7 180.7 %all-gather.8.cloned.1.call-start = ((), (), s32[]{:S(2)}) async-start(), calls=%async_computation.3 | async-start | bytes 6684672 | tf_op jit(solution)/shard_map/all_gather | solution.py:85
  9.4 275.1 %reduce-scatter.2.cloned.1.call-start = ((), (), s32[]{:S(2)}) async-start(), calls=%async_computation.4 | async-start | bytes 6291456 | tf_op jit(solution)/shard_map/reduce_scatter | solution.py:148
  27.1 3.5 %copy-start.2 = (bf16[1024,2048]{1,0:T(8,128)(2,1)S(1)}, bf16[1024,2048]{1,0:T(8,128)(2,1)}, u32[]{:S(2)}) copy-start(bf16[1024,2048]{1,0:T(8,128)(2,1)} %all-gather.4.cloned.1.call-done) | copy-start | bytes 12582916
  99.1 2.4 copy-start.3
  101.5 1.5 copy-start.10
  189.4 10.2 %copy-start.6 = (bf16[16,1536]{1,0:T(8,128)(2,1)S(1)}, bf16[16,1536]{1,0:T(8,128)(2,1)}, u32[]{:S(2)}) copy-start(bf16[16,1536]{1,0:T(8,128)(2,1)} %get-tuple-element.6) | copy-start | bytes 147460
  189.4 10.2 %copy-start.7 = (bf16[16,1536]{1,0:T(8,128)(2,1)S(1)}, bf16[16,1536]{1,0:T(8,128)(2,1)}, u32[]{:S(2)}) copy-start(bf16[16,1536]{1,0:T(8,128)(2,1)} %get-tuple-element.7) | copy-start | bytes 147460
  189.4 10.2 %copy-start.8 = (bf16[16,1536]{1,0:T(8,128)(2,1)S(1)}, bf16[16,1536]{1,0:T(8,128)(2,1)}, u32[]{:S(2)}) copy-start(bf16[16,1536]{1,0:T(8,128)(2,1)} %get-tuple-element.8) | copy-start | bytes 147460
  189.4 10.2 %copy-start.9 = (bf16[16,1536]{1,0:T(8,128)(2,1)S(1)}, bf16[16,1536]{1,0:T(8,128)(2,1)}, u32[]{:S(2)}) copy-start(bf16[16,1536]{1,0:T(8,128)(2,1)} %get-tuple-element.9) | copy-start | bytes 147460
  203.3 6.7 %copy-start.5 = (f32[1024,32]{0,1:T(8,128)S(1)}, f32[1024,32]{0,1:T(8,128)}, u32[]{:S(2)}) copy-start(f32[1024,32]{0,1:T(8,128)} %get-tuple-element.17) | copy-start | bytes 393220
  273.0 1.2 copy-start.4
  274.2 14.8 %copy-start.1 = (bf16[512,2048]{1,0:T(8,128)(2,1)S(1)}, bf16[512,2048]{1,0:T(8,128)(2,1)}, u32[]{:S(2)}) copy-start(bf16[512,2048]{1,0:T(8,128)(2,1)} %param.17) | copy-start | bytes 6291460
Sparse Core Ops, SparseCore 0:
  9.6 15.0 all-gather.3
  27.4 65.6 all-gather.5
  95.8 93.5 all-gather.7
  273.2 11.3 reduce-scatter.1
where the time goes:
time: 297 us; the launch traced here: 296 us
  waiting for transfers between devices  150 us (51%)
  matrix products  86.5 us (29%)
  between operations  19.1 us (6%)
  local copies, waits for them, and re-layouts  18.5 us (6%)
  other arithmetic  17.5 us (6%)
  blocking collectives  3.59 us (1%)
    all_gather x1, waiting for transfers between devices, body(): lax.all_gather(q_weight, 'wide', axis=0, tiled=True)  83.6 us
    all_gather x1, waiting for transfers between devices, body(): lax.all_gather(kva_weight, 'wide', axis=0, tiled=True)  55.3 us
    sub x1, matrix products, body(): expo = jnp.exp(scores - top)  26.8 us
    dot_general x1, matrix products, body(): jnp.einsum('qhd,kd->hqk', query_vectors[..., NOPE:], key_rope, preferred_...  13.4 us
    dot_general x1, matrix products, body(): jnp.einsum('hqk,khd->qhd', weights, values, preferred_element_type=jnp.fl...  12.7 us
    dot_general x1, matrix products, body(): jnp.dot(normed, lax.all_gather(q_weight, 'wide', axis=0, tiled=True), pre...  10.1 us
    reduce_scatter x1, waiting for transfers between devices, body(): lax.psum_scatter(partial_out.astype(jnp.bfloat16), 'narrow', scatter_dime...  9.2 us
    dot_general x1, matrix products, body(): jnp.dot(attended, o_weight, preferred_element_type=jnp.float32)  8.29 us
  transfers between devices with their start and end apart: 4, of which 3 were waited for; matrix products, arithmetic and copies ran while one was open for 11% of the time, Pallas kernels for 0%

commit v1 on v0

v1 whole, which is shorter than its diff:
```python
import functools
import math

import jax
import jax.numpy as jnp
from jax import lax
from jax.experimental import pallas as pl
from jax.experimental.pallas import tpu as pltpu
from jax.sharding import PartitionSpec as P

NOPE = 128
ROPE = 64
VDIM = 128
LATENT = 512
RANK = 16
LMAX = 512

EPS = 1e-06
THETA = 50000.0
ADAPTER_SCALE = 2.0

PAIR = 2 * (NOPE + ROPE)
TILE = 256
BAND = TILE + LMAX
MESH = pl.DeviceIdType.MESH
F32 = jnp.float32
BF16 = jnp.bfloat16


def axes_of(wide):
    side = math.isqrt(wide // 4)
    if wide % 4 == 0 and side * side * 4 == wide:
        return 4, side, side
    return wide, 1, 1


def iota(shape, dim):
    return lax.broadcasted_iota(jnp.int32, shape, dim)


def permute_pair(block):
    return jnp.concatenate(
        [
            block[:, :NOPE],
            block[:, NOPE + ROPE : 2 * NOPE + ROPE],
            block[:, NOPE : NOPE + ROPE],
            block[:, 2 * NOPE + ROPE :],
        ],
        axis=1,
    )


def turn(values, cosine, sine):
    low_half = (iota(values.shape, 1) & (ROPE - 1)) < ROPE // 2
    swapped = jnp.where(
        low_half,
        pltpu.roll(values, 2 * ROPE - ROPE // 2, 1),
        pltpu.roll(values, ROPE // 2, 1),
    )
    return values * cosine + swapped * sine


def kernel(
    dims,
    tokens,
    attn_gain,
    q_weight,
    kva_weight,
    kv_gain,
    kvb_weight,
    o_weight,
    adapter_down,
    adapter_up,
    lengths,
    ids,
    slots,
    hidden,
    cache,
    xbuf,
    normed,
    qstage,
    wq,
    wk,
    kvb,
    obuf,
    down,
    up,
    upsel,
    expanded,
    krot,
    latbuf,
    att,
    sendbuf,
    recvbuf,
    hbuf,
    bias,
    cosines,
    sines,
    low,
    low_other,
    spread,
    load_sem,
    store_sem,
    p1_send,
    p1_recv,
    p2_send,
    p2_recv,
    p3_send,
    p3_recv,
    core_send,
    core_recv,
    out_send,
    out_recv,
):
    nz, ny, nx = dims
    chunks = wq.shape[0]
    rows, half = tokens.shape
    tiles = rows // TILE
    depth = q_weight.shape[0]
    hd = depth // 2
    prompts = lengths.shape[1]
    wide = lax.axis_index("wide")
    core = lax.axis_index("narrow")
    x = wide % nx
    y = (wide // nx) % ny
    z = wide // (nx * ny)
    sib = 1 - core

    def at(zz, yy, xx):
        return (zz * ny + yy) * nx + xx

    def z_peer(d):
        return (at((z + d) % nz, y, x), core)

    def p_at(d):
        yy = (y + d * core) % ny
        xx = (x + d * (1 - core)) % nx
        return yy, xx

    def p_peer(d):
        yy, xx = p_at(d)
        return (at(z, yy, xx), core)

    def q_at(d):
        yy = (y + d * (1 - core)) % ny
        xx = (x + d * core) % nx
        return yy, xx

    def q_peer(d):
        yy, xx = q_at(d)
        return (at(z, yy, xx), core)

    def remote(src, dst, send, recv, device):
        return pltpu.make_async_remote_copy(
            src_ref=src, dst_ref=dst, send_sem=send, recv_sem=recv,
            device_id=device, device_id_type=MESH,
        )

    def piece(k, zz, yy, xx):
        if k == 0:
            return wk.at[zz, yy, xx, core]
        return wq.at[k - 1, zz, yy, xx]

    def p1(k, d):
        mine = piece(k, z, y, x)
        return remote(mine, mine, p1_send.at[k, d - 1], p1_recv.at[k, d - 1], z_peer(d))

    def p1_got(k, d):
        theirs = piece(k, (z - d + nz) % nz, y, x)
        return remote(theirs, theirs, p1_send.at[k, d - 1], p1_recv.at[k, d - 1], z_peer(d))

    def start_p1(k):
        for d in range(1, nz):
            p1(k, d).start()

    def wait_p1(k):
        for d in range(1, nz):
            p1_got(k, d).wait_recv()

    def column(k, yy, xx):
        return piece(k, slice(None), yy, xx)

    def start_p2(k):
        for d in range(1, nx):
            mine = column(k, y, x)
            remote(mine, mine, p2_send.at[k, d - 1], p2_recv.at[k, d - 1], p_peer(d)).start()

    def wait_p2(k):
        for d in range(1, nx):
            theirs = column(k, *p_at(nx - d))
            remote(theirs, theirs, p2_send.at[k, d - 1], p2_recv.at[k, d - 1], p_peer(d)).wait_recv()

    def plane(k, d, first):
        yy, xx = q_at(d)
        if first:
            return piece(k, slice(None), yy, slice(None))
        return piece(k, slice(None), slice(None), xx)

    def each_core(body):
        @pl.when(core == 0)
        def _():
            body(True)

        @pl.when(core == 1)
        def _():
            body(False)

    def start_p3(k):
        def body(first):
            for d in range(1, nx):
                mine = plane(k, 0, first)
                remote(mine, mine, p3_send.at[k, d - 1], p3_recv.at[k, d - 1], q_peer(d)).start()

        if nx > 1:
            each_core(body)

    def wait_p3(k):
        def body(first):
            for d in range(1, nx):
                theirs = plane(k, nx - d, first)
                remote(theirs, theirs, p3_send.at[k, d - 1], p3_recv.at[k, d - 1], q_peer(d)).wait_recv()

        if nx > 1:
            each_core(body)

    def drain(k):
        for d in range(1, nz):
            p1(k, d).wait_send()
        for d in range(1, nx):
            mine = column(k, y, x)
            remote(mine, mine, p2_send.at[k, d - 1], p2_recv.at[k, d - 1], p_peer(d)).wait_send()

        def body(first):
            for d in range(1, nx):
                mine = plane(k, 0, first)
                remote(mine, mine, p3_send.at[k, d - 1], p3_recv.at[k, d - 1], q_peer(d)).wait_send()

        if nx > 1:
            each_core(body)

    loads = [
        pltpu.make_async_copy(q_weight, qstage, load_sem.at[0]),
        pltpu.make_async_copy(
            kva_weight.at[pl.ds(pl.multiple_of(core * hd, hd), hd)],
            wk.at[z, y, x, core],
            load_sem.at[1],
        ),
        pltpu.make_async_copy(tokens, xbuf.at[core], load_sem.at[2]),
        pltpu.make_async_copy(adapter_down, down, load_sem.at[3]),
        pltpu.make_async_copy(kvb_weight, kvb, load_sem.at[4]),
        pltpu.make_async_copy(adapter_up, up, load_sem.at[5]),
        pltpu.make_async_copy(o_weight.at[:, pl.ds(0, half)], obuf.at[0], load_sem.at[6]),
        pltpu.make_async_copy(o_weight.at[:, pl.ds(half, half)], obuf.at[1], load_sem.at[7]),
    ]
    for load in loads:
        load.start()

    barrier = pltpu.get_barrier_semaphore()
    peers = [(wide, sib)]
    peers += [z_peer(d) for d in range(1, nz)]
    peers += [p_peer(d) for d in range(1, nx)]
    peers += [q_peer(d) for d in range(1, nx)]
    for peer in peers:
        pl.semaphore_signal(barrier, inc=1, device_id=peer, device_id_type=MESH)
    loads[0].wait()
    for j in range(chunks):
        wq[j, z, y, x] = permute_pair(qstage[:, j * PAIR : (j + 1) * PAIR])
    loads[1].wait()
    pl.semaphore_wait(barrier, len(peers))

    start_p1(0)
    loads[2].wait()
    sib_tokens = remote(xbuf.at[core], xbuf.at[core], core_send.at[0], core_recv.at[0], (wide, sib))
    sib_tokens.start()
    for k in range(1, chunks + 1):
        start_p1(k)

    ends = []
    total = jnp.int32(0)
    for j in range(prompts):
        total = total + lengths[0, j]
        ends.append(total)
    starts = [ends[j] - lengths[0, j] for j in range(prompts)]

    def prompt_of(index):
        found = jnp.zeros_like(index)
        for end in ends:
            found = found + (index >= end).astype(jnp.int32)
        return found

    def by_prompt(prompt, values):
        out = jnp.zeros_like(prompt)
        for j, value in enumerate(values):
            out = jnp.where(prompt == j, value, out)
        return out

    def tile(i):
        return pl.ds(pl.multiple_of(i * TILE, TILE), TILE)

    def band_start(i):
        return jnp.maximum(i - LMAX // TILE, 0) * TILE

    def tables(i, _):
        index = iota((TILE, 128), 0) + i * TILE
        position = index - by_prompt(prompt_of(index), starts)
        lane = iota((TILE, 128), 1)
        step = (lane & (ROPE // 2 - 1)).astype(F32)
        freqs = jnp.exp(-math.log(THETA) * 2.0 * step / ROPE)
        angle = position.astype(F32) * freqs
        cosines[tile(i)] = jnp.cos(angle)
        sine = jnp.sin(angle)
        sines[tile(i)] = jnp.where((lane & (ROPE - 1)) < ROPE // 2, -sine, sine)
        query = iota((TILE, BAND), 0) + i * TILE
        key = iota((1, BAND), 1) + band_start(i)
        same = prompt_of(iota((TILE, 1), 0) + i * TILE) == prompt_of(key)
        bias[i] = jnp.where(same & (key <= query), 0.0, -1e30).astype(F32)
        return 0

    lax.fori_loop(0, tiles, tables, 0)
    wait_p1(0)
    start_p2(0)

    sib_tokens.wait_recv()
    gain = attn_gain[...].astype(F32)

    def norm(i, _):
        left = xbuf[0, tile(i)].astype(F32)
        right = xbuf[1, tile(i)].astype(F32)
        total_sq = jnp.sum(left * left, -1, keepdims=True) + jnp.sum(right * right, -1, keepdims=True)
        factor = lax.rsqrt(total_sq / (2 * half) + EPS)
        normed[tile(i), :half] = (left * factor * gain[:, :half]).astype(BF16)
        normed[tile(i), half:] = (right * factor * gain[:, half:]).astype(BF16)
        return 0

    lax.fori_loop(0, tiles, norm, 0)
    wait_p2(0)
    start_p3(0)
    wait_p1(1)
    start_p2(1)

    loads[3].wait()
    owned = down.shape[1]

    def slot_of(j):
        found = jnp.int32(0)
        for n in range(slots.shape[0]):
            found = found + jnp.where(ids[0, j] == n, slots[n], 0)
        return found - core * (owned // RANK)

    slot_values = [slot_of(j) for j in range(prompts)]

    def lowrank(i, _):
        every = jnp.dot(normed[tile(i)], down[...], preferred_element_type=F32)
        index = iota((TILE, 1), 0) + i * TILE
        slot = by_prompt(prompt_of(index), slot_values)
        kept = jnp.where((iota((TILE, owned), 1) >> 4) == slot, every, 0.0).astype(BF16)
        fold = ((iota((owned, 128), 0) & (RANK - 1)) == (iota((owned, 128), 1) & (RANK - 1)))
        low[tile(i)] = jnp.dot(
            kept, fold.astype(F32).astype(BF16), preferred_element_type=F32
        ).astype(BF16)
        return 0

    lax.fori_loop(0, tiles, lowrank, 0)
    sib_low = remote(low, low_other, core_send.at[1], core_recv.at[1], (wide, sib))
    sib_low.start()

    wait_p3(0)
    own_kva = wk.at[:, :, :, core]
    sib_kva = remote(own_kva, own_kva, core_send.at[2], core_recv.at[2], (wide, sib))
    sib_kva.start()
    wait_p2(1)
    start_p3(1)
    wait_p1(2)
    start_p2(2)

    loads[5].wait()
    row = iota((128, up.shape[0]), 0)
    wanted = jnp.full_like(row, -1)
    for n in range(prompts):
        wanted = jnp.where((row >> 4) == n, ids[0, n] * RANK + (row & (RANK - 1)), wanted)
    picker = (iota(row.shape, 1) == wanted).astype(F32).astype(BF16)
    for j in range(chunks):
        picked = jnp.dot(picker, up[:, j * PAIR : (j + 1) * PAIR], preferred_element_type=F32)
        upsel[j] = permute_pair(picked.astype(BF16))
    sib_low.wait_recv()

    def place(i, _):
        both = low[tile(i)].astype(F32) + low_other[tile(i)].astype(F32)
        prompt = prompt_of(iota((TILE, 128), 0) + i * TILE)
        spread[tile(i)] = jnp.where((iota((TILE, 128), 1) >> 4) == prompt, both, 0.0).astype(BF16)
        return 0

    lax.fori_loop(0, tiles, place, 0)

    loads[4].wait()
    theirs = wk.at[:, :, :, sib]
    remote(theirs, theirs, core_send.at[2], core_recv.at[2], (wide, sib)).wait_recv()
    gain2 = kv_gain[...].astype(F32)

    def keys(i, _):
        pre = jnp.dot(
            normed[tile(i)], wk[...].reshape(nz * ny * nx * depth, LATENT + ROPE),
            preferred_element_type=F32,
        )
        body = pre[:, :LATENT]
        factor = lax.rsqrt(jnp.mean(body * body, -1, keepdims=True) + EPS)
        latent = (body * factor * gain2).astype(BF16)
        rope = pre[:, LATENT:]
        rope = turn(jnp.concatenate([rope, rope], axis=1), cosines[tile(i)], sines[tile(i)])
        rope = rope.astype(BF16)
        krot[tile(i)] = rope
        latbuf[tile(i), :LATENT] = latent
        latbuf[tile(i), LATENT:] = rope[:, :ROPE]
        wide_kv = jnp.dot(latent, kvb[...], preferred_element_type=F32).astype(BF16)
        for h in range(2 * chunks):
            expanded[h, tile(i)] = wide_kv[:, h * 256 : (h + 1) * 256]
        return 0

    lax.fori_loop(0, tiles, keys, 0)
    save_cache = pltpu.make_async_copy(latbuf, cache, store_sem.at[tiles])
    save_cache.start()

    scale = (1.0 / math.sqrt(NOPE + ROPE)) * math.log2(math.e)

    def attend(j):
        def step(i, _):
            query = jnp.dot(
                normed[tile(i)], wq[j].reshape(nz * ny * nx * depth, PAIR),
                preferred_element_type=F32,
            )
            query = query + ADAPTER_SCALE * jnp.dot(
                spread[tile(i)], upsel[j], preferred_element_type=F32
            )
            rope = turn(query[:, 2 * NOPE :], cosines[tile(i)], sines[tile(i)])
            lane = iota(rope.shape, 1)
            band = pl.ds(pl.multiple_of(band_start(i), TILE), BAND)
            key_rope = krot[band]
            for h in range(2):
                own = (lane >= h * ROPE) & (lane < (h + 1) * ROPE)
                full = jnp.concatenate(
                    [query[:, h * NOPE : (h + 1) * NOPE], jnp.where(own, rope, 0.0)], axis=1
                ).astype(BF16)
                pair = expanded[2 * j + h, band]
                key = jnp.concatenate([pair[:, :NOPE], key_rope], axis=1)
                scores = lax.dot_general(
                    full, key, (((1,), (1,)), ((), ())), preferred_element_type=F32
                )
                scores = scores * scale + bias[i]
                expo = jnp.exp2(scores - jnp.max(scores, -1, keepdims=True))
                weights = (expo * (1.0 / jnp.sum(expo, -1, keepdims=True))).astype(BF16)
                out = jnp.dot(weights, pair[:, NOPE:], preferred_element_type=F32)
                att[j, tile(i), h * VDIM : (h + 1) * VDIM] = out.astype(BF16)
            return 0

        lax.fori_loop(0, tiles, step, 0)

    for j in range(chunks):
        k = j + 1
        if k + 1 <= chunks:
            wait_p2(k + 1)
            start_p3(k + 1)
        if k + 2 <= chunks:
            wait_p1(k + 2)
            start_p2(k + 2)
        wait_p3(k)
        attend(j)

    loads[6].wait()
    loads[7].wait()

    def heads_of(i):
        return jnp.concatenate([att[j, tile(i)] for j in range(chunks)], axis=1)

    def give(i):
        return remote(sendbuf.at[i], recvbuf.at[i], out_send.at[i], out_recv.at[i], (wide, sib))

    def project_away(i, _):
        part = jnp.dot(heads_of(i), obuf[sib], preferred_element_type=F32)
        sendbuf[i] = part.astype(BF16)
        give(i).start()
        return 0

    lax.fori_loop(0, tiles, project_away, 0)

    def save(i):
        return pltpu.make_async_copy(hbuf.at[i], hidden.at[tile(i)], store_sem.at[i])

    def project_here(i, _):
        part = jnp.dot(heads_of(i), obuf[core], preferred_element_type=F32)
        part = part.astype(BF16).astype(F32)
        give(i).wait_recv()
        part = part + recvbuf[i].astype(F32)
        hbuf[i] = (xbuf[core, tile(i)].astype(F32) + part).astype(BF16)
        save(i).start()
        return 0

    lax.fori_loop(0, tiles, project_here, 0)

    for k in range(chunks + 1):
        drain(k)
    sib_tokens.wait_send()
    sib_low.wait_send()
    sib_kva.wait_send()
    save_cache.wait()
    for i in range(tiles):
        give(i).wait_send()
        save(i).wait()


def body(
    wide,
    tokens,
    attn_gain,
    q_weight,
    kva_weight,
    kv_gain,
    kvb_weight,
    o_weight,
    adapter_down,
    adapter_up_weight,
    lengths,
    adapter_ids,
    adapter_slot,
):
    dims = axes_of(wide)
    nz, ny, nx = dims
    rows, half = tokens.shape
    depth = q_weight.shape[0]
    chunks = q_weight.shape[1] // PAIR
    tiles = rows // TILE
    heads = o_weight.shape[0] // VDIM
    any_spec = pl.BlockSpec(memory_space=pl.ANY)
    vmem = pl.BlockSpec(memory_space=pltpu.VMEM)
    smem = pl.BlockSpec(memory_space=pltpu.SMEM)
    dma = pltpu.SemaphoreType.DMA
    V = pltpu.VMEM
    line = max(nx - 1, 1)
    return pl.pallas_call(
        functools.partial(kernel, dims),
        out_shape=(
            jax.ShapeDtypeStruct((rows, half), BF16),
            jax.ShapeDtypeStruct((rows, LATENT + ROPE), BF16),
        ),
        in_specs=[any_spec, vmem, any_spec, any_spec, vmem]
        + [any_spec] * 4
        + [smem] * 3,
        out_specs=(any_spec, any_spec),
        scratch_shapes=[
            V((2, rows, half), BF16),
            V((rows, 2 * half), BF16),
            V(q_weight.shape, BF16),
            V((chunks, nz, ny, nx, depth, PAIR), BF16),
            V((nz, ny, nx, 2, depth // 2, LATENT + ROPE), BF16),
            V(kvb_weight.shape, BF16),
            V((2, o_weight.shape[0], half), BF16),
            V(adapter_down.shape, BF16),
            V(adapter_up_weight.shape, BF16),
            V((chunks, 128, PAIR), BF16),
            V((heads, rows, NOPE + VDIM), BF16),
            V((rows, 2 * ROPE), BF16),
            V((rows, LATENT + ROPE), BF16),
            V((chunks, rows, 2 * VDIM), BF16),
            V((tiles, TILE, half), BF16),
            V((tiles, TILE, half), BF16),
            V((tiles, TILE, half), BF16),
            V((tiles, TILE, BAND), F32),
            V((rows, 2 * ROPE), F32),
            V((rows, 2 * ROPE), F32),
            V((rows, 128), BF16),
            V((rows, 128), BF16),
            V((rows, 128), BF16),
            dma((8,)),
            dma((tiles + 1,)),
            dma((chunks + 1, nz - 1)),
            dma((chunks + 1, nz - 1)),
            dma((chunks + 1, line)),
            dma((chunks + 1, line)),
            dma((chunks + 1, line)),
            dma((chunks + 1, line)),
            dma((3,)),
            dma((3,)),
            dma((tiles,)),
            dma((tiles,)),
        ],
        compiler_params=pltpu.CompilerParams(
            collective_id=0, has_side_effects=True, vmem_limit_bytes=62 * 1024 * 1024
        ),
        name="latent_block",
    )(
        tokens,
        attn_gain.reshape(1, -1),
        q_weight,
        kva_weight,
        kv_gain.reshape(1, -1),
        kvb_weight,
        o_weight,
        adapter_down,
        adapter_up_weight,
        lengths,
        adapter_ids,
        adapter_slot,
    )


def solution(mesh):
    return jax.shard_map(
        functools.partial(body, mesh.shape["wide"]),
        mesh=mesh,
        in_specs=(
            P("wide", "narrow"),
            P(),
            P("wide", "narrow"),
            P("wide", None),
            P(),
            P(None, "narrow"),
            P("narrow", None),
            P(None, "narrow"),
            P(None, "narrow"),
            P("wide", None),
            P("wide", None),
            P(),
        ),
        out_specs=(P("wide", "narrow"), P("wide", None)),
        check_vma=False,
    )
```

time: 297 us -> 113 us (0.38)
  waiting for transfers between devices: 150 us -> 0 us
  Pallas kernels: 0 us -> 104 us
  matrix products: 86.5 us -> 0 us
  between operations: 19.1 us -> 0.65 us
  other arithmetic: 17.5 us -> 0 us
  local copies, waits for them, and re-layouts: 18.5 us -> 8.12 us
  blocking collectives: 3.59 us -> 0 us
    all_gather x3 -> x0, waiting for transfers between devices: 139 us -> none  [the longest x1 83.6 us: body(): lax.all_gather(q_weight, 'wide', axis=0, tiled=True)]
    pallas_call x0 -> x1, Pallas kernels: none -> 104 us  [body(): pl.pallas_call(functools.partial(kernel, dims), out_shape=(jax.ShapeDtype...]
    dot_general x8 -> x0, matrix products: 59.7 us -> none  [the longest x1 13.4 us: body(): jnp.einsum('qhd,kd->hqk', query_vectors[..., NOPE:], key_rope, preferred_...]
    sub x1 -> x0, matrix products: 26.8 us -> none  [body(): expo = jnp.exp(scores - top)]
    reduce_scatter x1 -> x0, waiting for transfers between devices: 9.2 us -> none  [body(): lax.psum_scatter(partial_out.astype(jnp.bfloat16), 'narrow', scatter_dime...]
    add x1 -> x0, local copies, waits for them, and re-layouts: 6.66 us -> none  [body(): query_vectors + ADAPTER_SCALE * jnp.dot(spread_rows, up_weight_rows, pref...]
    convert_element_type x7 -> x0, other arithmetic: 6.13 us -> none  [the longest x1 4.5 us: body(): hidden = (tokens.astype(jnp.float32) + projected).astype(jnp.bfloat16)]
    dynamic_slice x2 -> x0, local copies, waits for them, and re-layouts: 5.17 us -> none  [the longest x1 3.54 us: pick_columns(): lax.dynamic_slice_in_dim(stored, first_slots[prompt_index] * RANK, RANK, 1)]
  transfers between devices with their start and end apart: 4 -> 0, of which waited for: 3 -> 0; matrix products, arithmetic and copies ran while one was open for 11% -> 0% of each run, Pallas kernels for 0% -> 0%
where the time goes in v1:
time: 113 us
  Pallas kernels  104 us (92%)
  local copies, waits for them, and re-layouts  8.12 us (7%)
    pallas_call x1, Pallas kernels, body(): pl.pallas_call(functools.partial(kernel, dims), out_shape=(jax.ShapeDtype...  104 us
    unnamed x4, local copies, waits for them, and re-layouts  3.04 us
    pallas_call x1, local copies, waits for them, and re-layouts, body(): pl.pallas_call(functools.partial(kernel, dims), out_shape=(jax.ShapeDtype...  2.52 us

profile of v1, /device:TPU:8, one launch (start us, length us, event | category | flops | bytes accessed | tf_op | source)
XLA Modules:
  0.0 112.7 jit_solution(9540521185465741150)
XLA Ops:
  0.6 1.3 %reshape.11.kv_gain = bf16[1,512]{1,0:T(2,128)(2,1)} reshape(bf16[512]{0:T(512)(128)(2,1)} %param.16) | data formatting | bytes 2048 | tf_op jit(solution)/shard_map/reshape | solution.py:594
  1.9 1.3 %reshape.10.attn_gain = bf16[1,2048]{1,0:T(2,128)(2,1)} reshape(bf16[2048]{0:T(1024)(128)(2,1)} %param.13) | data formatting | bytes 8192 | tf_op jit(solution)/shard_map/reshape | solution.py:591
  3.2 1.7 %copy.14.kva_weight = bf16[128,576]{1,0:T(8,128)(2,1)} copy(bf16[128,576]{0,1:T(8,128)(2,1)} %param.15) | data formatting | bytes 294912 | tf_op args[3]
  4.9 103.9 %latent_block.1 = (bf16[1024,1024]{1,0:T(8,128)(2,1)}, bf16[1024,576]{1,0:T(8,128)(2,1)}) custom-call(bf16[1024,1024]{1,0:T(8,128)(2,1)} %tokens.1, bf16[1,2048]{1,0:T(2,128)(2,1)} %reshape.10.attn_gain, bf16[128,1536]{1,0:T(8,128)(2,1)} %q_weight.1, bf16[128,576]{1,0:T(8,128)(2,1)} %copy.14.kva_weight, bf16[1,512]{1,0:T(2,128)(2,1)} %reshape.11.kv_gain, ...), custom_call_target="tpu_custom_call" | custom-call | tf_op jit(solution)/shard_map/latent_block/pallas_call | solution.py:538
  108.8 0.0 copy-start
  108.9 2.5 %copy.15 = bf16[1024,576]{0,1:T(8,128)(2,1)} copy(bf16[1024,576]{1,0:T(8,128)(2,1)} %get-tuple-element.3) | data formatting | bytes 2359296 | tf_op jit(solution)/shard_map/latent_block/pallas_call | solution.py:538
  111.4 0.0 copy-done
  111.4 1.3 %copy.17 = bf16[1024,1024]{1,0:T(8,128)(2,1)} copy(bf16[1024,1024]{1,0:T(8,128)(2,1)S(1)} %copy-done) | data formatting | bytes 4194304
Async XLA Ops:
  108.8 2.5 %copy-start = (bf16[1024,1024]{1,0:T(8,128)(2,1)S(1)}, bf16[1024,1024]{1,0:T(8,128)(2,1)}, u32[]{:S(2)}) copy-start(bf16[1024,1024]{1,0:T(8,128)(2,1)} %get-tuple-element.6) | copy-start | bytes 6291460

commit v2 on v1

--- a/solution.py
+++ b/solution.py
@@ -272,8 +272,6 @@
     loads[2].wait()
     sib_tokens = remote(xbuf.at[core], xbuf.at[core], core_send.at[0], core_recv.at[0], (wide, sib))
     sib_tokens.start()
-    for k in range(1, chunks + 1):
-        start_p1(k)
 
     ends = []
     total = jnp.int32(0)
@@ -316,12 +314,18 @@
         bias[i] = jnp.where(same & (key <= query), 0.0, -1e30).astype(F32)
         return 0
 
-    lax.fori_loop(0, tiles, tables, 0)
     wait_p1(0)
     start_p2(0)
-
+    start_p1(1)
+    lax.fori_loop(0, tiles, tables, 0)
+
+    wait_p2(0)
+    start_p3(0)
+    wait_p1(1)
+    start_p2(1)
+    start_p1(2)
     sib_tokens.wait_recv()
-    gain = attn_gain[...].astype(F32)
+    gain = attn_gain[...].astype(F32).reshape(1, 2 * half)
 
     def norm(i, _):
         left = xbuf[0, tile(i)].astype(F32)
@@ -333,10 +337,6 @@
         return 0
 
     lax.fori_loop(0, tiles, norm, 0)
-    wait_p2(0)
-    start_p3(0)
-    wait_p1(1)
-    start_p2(1)
 
     loads[3].wait()
     owned = down.shape[1]
@@ -372,6 +372,7 @@
     start_p3(1)
     wait_p1(2)
     start_p2(2)
+    start_p1(3)
 
     loads[5].wait()
     row = iota((128, up.shape[0]), 0)
@@ -395,7 +396,7 @@
     loads[4].wait()
     theirs = wk.at[:, :, :, sib]
     remote(theirs, theirs, core_send.at[2], core_recv.at[2], (wide, sib)).wait_recv()
-    gain2 = kv_gain[...].astype(F32)
+    gain2 = kv_gain[...].astype(F32).reshape(1, LATENT)
 
     def keys(i, _):
         pre = jnp.dot(
@@ -462,6 +463,8 @@
         if k + 2 <= chunks:
             wait_p1(k + 2)
             start_p2(k + 2)
+        if k + 3 <= chunks:
+            start_p1(k + 3)
         wait_p3(k)
         attend(j)
 
@@ -588,10 +591,10 @@
         name="latent_block",
     )(
         tokens,
-        attn_gain.reshape(1, -1),
+        attn_gain,
         q_weight,
         kva_weight,
-        kv_gain.reshape(1, -1),
+        kv_gain,
         kvb_weight,
         o_weight,
         adapter_down,

time: 113 us -> 104 us (0.920)
  Pallas kernels: 104 us -> 97.1 us
  local copies, waits for them, and re-layouts: 8.12 us -> 5.56 us
    pallas_call x1, Pallas kernels: 104 us -> 97.1 us  [body(): pl.pallas_call(functools.partial(kernel, dims), out_shape=(jax.ShapeDtype...]
    reshape x2 -> x0, local copies, waits for them, and re-layouts: 2.56 us -> none  [the longest x1 1.29 us: body(): attn_gain.reshape(1, -1)]
where the time goes in v2:
time: 104 us; the launch traced here: 103 us
  Pallas kernels  97.1 us (93%)
  local copies, waits for them, and re-layouts  5.56 us (5%)
    pallas_call x1, Pallas kernels, body(): pl.pallas_call(functools.partial(kernel, dims), out_shape=(jax.ShapeDtype...  97.1 us
    unnamed x4, local copies, waits for them, and re-layouts  3.04 us
    pallas_call x1, local copies, waits for them, and re-layouts, body(): pl.pallas_call(functools.partial(kernel, dims), out_shape=(jax.ShapeDtype...  2.52 us

profile of v2, /device:TPU:8, one launch (start us, length us, event | category | flops | bytes accessed | tf_op | source)
XLA Modules:
  0.0 103.3 jit_solution(1429823540712253020)
XLA Ops:
  0.6 1.7 %copy.14.kva_weight = bf16[128,576]{1,0:T(8,128)(2,1)} copy(bf16[128,576]{0,1:T(8,128)(2,1)} %param.15) | data formatting | bytes 294912 | tf_op args[3]
  2.3 97.1 %latent_block.1 = (bf16[1024,1024]{1,0:T(8,128)(2,1)}, bf16[1024,576]{1,0:T(8,128)(2,1)}) custom-call(bf16[1024,1024]{1,0:T(8,128)(2,1)} %tokens.1, bf16[2048]{0:T(1024)(128)(2,1)} %attn_gain.1, bf16[128,1536]{1,0:T(8,128)(2,1)} %q_weight.1, bf16[128,576]{1,0:T(8,128)(2,1)} %copy.14.kva_weight, bf16[512]{0:T(512)(128)(2,1)} %kv_gain.1, ...), custom_call_target="tpu_custom_call" | custom-call | tf_op jit(solution)/shard_map/latent_block/pallas_call | solution.py:541
  99.4 0.0 copy-start
  99.4 2.5 %copy.15 = bf16[1024,576]{0,1:T(8,128)(2,1)} copy(bf16[1024,576]{1,0:T(8,128)(2,1)} %get-tuple-element.3) | data formatting | bytes 2359296 | tf_op jit(solution)/shard_map/latent_block/pallas_call | solution.py:541
  101.9 0.0 copy-done
  101.9 1.3 %copy.17 = bf16[1024,1024]{1,0:T(8,128)(2,1)} copy(bf16[1024,1024]{1,0:T(8,128)(2,1)S(1)} %copy-done) | data formatting | bytes 4194304
Async XLA Ops:
  99.4 2.5 %copy-start = (bf16[1024,1024]{1,0:T(8,128)(2,1)S(1)}, bf16[1024,1024]{1,0:T(8,128)(2,1)}, u32[]{:S(2)}) copy-start(bf16[1024,1024]{1,0:T(8,128)(2,1)} %get-tuple-element.6) | copy-start | bytes 6291460
